TPU v7x, 256 devices: a whole 4x4x8 slice. The times are simulated.
256 devices in a mesh: ctx: 16 (over x_hi, y, core), exp: 16 (over z, x_lo).
Axes of the slice: x: 4 (x_hi: 2, x_lo: 2; x = x_hi * 2 + x_lo), y: 4, z: 8, core: 2. Of those that a mesh axis runs over, the one named last changes fastest.
Arguments:
- queries: bfloat16 [2048, 12288], P('ctx', 'exp'), may hold values from -100 to 100
- kv_latent: bfloat16 [2048, 576], P('ctx'), may hold values from -8 to 8
- kv_up: bfloat16 [512, 16384], P(None, 'exp'), may hold values from -0.25 to 0.25
- out_proj: bfloat16 [8192, 7168], P('exp', 'ctx'), may hold values from -0.0625 to 0.0625
- residual: bfloat16 [2048, 7168], P(('ctx', 'exp')), may hold values from -6 to 6
- norm_gain: float32 [7168], replicated, may hold values from 0.1 to 1.9
- routes: int32 [2048, 4], P(('ctx', 'exp')), may hold values from 0 to 31, all different within a row; in each aligned block of 8 rows (0 to 7, 8 to 15, ...) at most 2 rows name the same one
- gate_scores: float32 [2048, 4], P(('ctx', 'exp')), may hold values from 0.05 to 1
- expert_gate_up: bfloat16 [16, 2, 7168, 2048], P('exp', None, None, 'ctx'), may hold values from -0.0625 to 0.0625
- expert_down: bfloat16 [16, 2048, 7168], P('exp', 'ctx'), may hold values from -0.1875 to 0.1875
- shared_gate_up: bfloat16 [2, 7168, 2048], P(None, None, 'ctx'), may hold values from -0.0625 to 0.0625
- shared_down: bfloat16 [2048, 7168], P('ctx'), may hold values from -0.125 to 0.125
Outputs:
- layer_out: bfloat16 [2048, 7168], P(('ctx', 'exp'))
Inputs may be any that keep to these rules, and one draw needn't show every extreme that they name: `routes`: each row names 4 different experts; in each aligned block of 8 rows (the rows of one device) no expert is named by more than 2 rows, a bound that some block reaches.
All inputs are finite; a program needn't handle non-finite values.
Results may differ from a plain program's by a relative error of at most 0.027.
Values may be sent and summed in bfloat16 or wider, within the bound.
No kernel may reach another device: no remote copies, remote signals or barrier semaphores. Data moves between devices by JAX's collectives and lax.ppermute only.
A program may use at most 128 MiB of HBM per device.

v0:
```python
import math

import jax
import jax.numpy as jnp
from jax import lax
from jax.sharding import PartitionSpec as P

D = 7168
NOPE = 128
ROPE = 64
VHD = 128
KVL = 512
TOPK = 4


def swiglu(row_block, gate_proj, up_proj):
    gate_part = jnp.dot(row_block, gate_proj, preferred_element_type=jnp.float32)
    up_part = jnp.dot(row_block, up_proj, preferred_element_type=jnp.float32)
    return (jax.nn.silu(gate_part) * up_part).astype(jnp.bfloat16)


def on_device(
    queries,
    kv_latent,
    kv_up,
    out_proj,
    residual,
    norm_gain,
    routes,
    gate_scores,
    expert_gate_up,
    expert_down,
    shared_gate_up,
    shared_down,
):
    ctx_count = lax.axis_size("ctx")
    exp_count = lax.axis_size("exp")
    tok_block = queries.shape[0]
    heads_local = queries.shape[1] // (NOPE + ROPE)
    seq_total = tok_block * ctx_count
    query_heads = queries.reshape(tok_block, heads_local, NOPE + ROPE)
    shard_piece = lax.all_gather(kv_latent, "ctx", axis=0, tiled=True)
    piece_rows = shard_piece.shape[0]
    expanded = jnp.dot(shard_piece[:, :KVL], kv_up, preferred_element_type=jnp.float32).astype(
        jnp.bfloat16
    )
    expanded = expanded.reshape(piece_rows, heads_local, NOPE + VHD)
    rope_part = jnp.broadcast_to(shard_piece[:, None, KVL:], (piece_rows, heads_local, ROPE))
    key_full = jnp.concatenate([expanded[:, :, :NOPE], rope_part], axis=2)
    block_scores = jnp.einsum(
        "qhc,khc->hqk", query_heads, key_full, preferred_element_type=jnp.float32
    ) / math.sqrt(NOPE + ROPE)
    value_all = expanded[:, :, NOPE:]
    query_pos = lax.axis_index("ctx") * tok_block + jnp.arange(tok_block, dtype=jnp.int32)
    key_pos = jnp.arange(seq_total, dtype=jnp.int32)
    allowed = (key_pos[None, :] <= query_pos[:, None])[None, :, :]
    row_max = jnp.max(jnp.where(allowed, block_scores, -jnp.inf), axis=2, keepdims=True)
    weights = jnp.exp(jnp.where(allowed, block_scores - row_max, -jnp.inf))
    probabilities = weights.astype(jnp.bfloat16)
    weighted_sum = jnp.einsum(
        "hqk,khv->qhv", probabilities, value_all, preferred_element_type=jnp.float32
    )
    normalizer = jnp.sum(weights, axis=2).T[:, :, None]
    attended = (
        (weighted_sum / normalizer).astype(jnp.bfloat16).reshape(tok_block, heads_local * VHD)
    )
    projected = jnp.dot(
        attended,
        lax.all_gather(out_proj, "ctx", axis=1, tiled=True),
        preferred_element_type=jnp.float32,
    ).astype(jnp.bfloat16)
    head_total = lax.psum_scatter(
        lax.optimization_barrier(projected).astype(jnp.float32).astype(jnp.bfloat16),
        "exp",
        scatter_dimension=0,
        tiled=True,
    ).astype(jnp.float32)
    hidden = (residual.astype(jnp.float32) + head_total).astype(jnp.bfloat16)
    hidden_f = hidden.astype(jnp.float32)
    normed = (
        hidden_f
        * lax.rsqrt(jnp.mean(hidden_f * hidden_f, axis=1, keepdims=True) + 1e-06)
        * norm_gain
    ).astype(jnp.bfloat16)
    tok_local = residual.shape[0]
    experts = 2 * exp_count
    capacity = min(tok_local, 2 * tok_local * TOPK // experts)
    flat_routes = routes.reshape(-1)
    expert_ids = jnp.arange(experts, dtype=jnp.int32)
    onehot = (flat_routes[:, None] == expert_ids[None, :]).astype(jnp.int32)
    rank_within = jnp.sum((jnp.cumsum(onehot, axis=0) - 1) * onehot, axis=1)
    slot_index = (flat_routes * capacity + rank_within).reshape(tok_local, TOPK)
    slot_ids = jnp.arange(experts * capacity, dtype=jnp.int32)
    matches = slot_index[None, :, :] == slot_ids[:, None, None]
    placement = jnp.any(matches, axis=2).astype(jnp.bfloat16)
    send_rows = jnp.dot(placement, normed, preferred_element_type=jnp.float32).astype(jnp.bfloat16)
    send_rows = send_rows.reshape(exp_count, 2, capacity, D)
    received = lax.all_to_all(send_rows, "exp", split_axis=0, concat_axis=0, tiled=True)
    by_half = jnp.transpose(received, (1, 0, 2, 3)).reshape(2, exp_count * capacity, D)
    routed_send = jnp.repeat(by_half, ctx_count // 2, axis=0)
    shared_send = jnp.broadcast_to(normed[None], (ctx_count, tok_local, D))
    routed_in, shared_in = (
        lax.all_to_all(routed_send, "ctx", split_axis=0, concat_axis=0, tiled=True),
        lax.all_to_all(shared_send, "ctx", split_axis=0, concat_axis=0, tiled=True),
    )
    routed_act = swiglu(routed_in.reshape(-1, D), expert_gate_up[0, 0], expert_gate_up[0, 1])
    routed_part = jnp.dot(routed_act, expert_down[0], preferred_element_type=jnp.float32).astype(
        jnp.bfloat16
    )
    routed_part = routed_part.reshape(ctx_count, exp_count * capacity, D)
    shared_act = swiglu(shared_in.reshape(-1, D), shared_gate_up[0], shared_gate_up[1])
    shared_part = jnp.dot(shared_act, shared_down, preferred_element_type=jnp.float32).astype(
        jnp.bfloat16
    )
    shared_part = shared_part.reshape(ctx_count, tok_local, D)
    back_routed, back_shared = (
        lax.all_to_all(routed_part, "ctx", split_axis=0, concat_axis=0, tiled=True),
        lax.all_to_all(shared_part, "ctx", split_axis=0, concat_axis=0, tiled=True),
    )
    summed_parts = (
        back_routed.astype(jnp.float32)
        .reshape(2, ctx_count // 2, exp_count, capacity, D)
        .sum(axis=1)
    )
    expert_out = jnp.transpose(summed_parts, (1, 0, 2, 3)).astype(jnp.bfloat16)
    returned = lax.all_to_all(expert_out, "exp", split_axis=0, concat_axis=0, tiled=True).reshape(
        experts * capacity, D
    )
    route_weight = 2.5 * gate_scores / jnp.sum(gate_scores, axis=1, keepdims=True)
    weight_table = jnp.sum(jnp.where(matches, route_weight[None, :, :], 0.0), axis=2).T
    routed_total = jnp.dot(
        weight_table, returned.astype(jnp.float32), precision=lax.Precision.HIGHEST
    )
    shared_total = back_shared.astype(jnp.float32).sum(axis=0)
    return (hidden_f + shared_total + routed_total).astype(jnp.bfloat16)


def solution(mesh):
    return jax.shard_map(
        on_device,
        mesh=mesh,
        in_specs=(
            P("ctx", "exp"),
            P("ctx", None),
            P(None, "exp"),
            P("exp", "ctx"),
            P(("ctx", "exp"), None),
            P(),
            P(("ctx", "exp"), None),
            P(("ctx", "exp"), None),
            P("exp", None, None, "ctx"),
            P("exp", "ctx", None),
            P(None, None, "ctx"),
            P("ctx", None),
        ),
        out_specs=P(("ctx", "exp"), None),
        check_vma=False,
    )
```

profile of v0, /device:TPU:24, one launch (start us, length us, event | category | flops | bytes accessed | tf_op | source)
XLA Modules:
  0.0 562.0 jit_solution(12175248104703348526)
XLA Ops:
  8.1 1.1 copy.41
  9.3 54.6 %all-gather.3.cloned.1.call-done = bf16[2048,576]{0,1:T(8,128)(2,1)} async-done(((bf16[128,576]{0,1:T(8,128)(2,1)}), bf16[2048,576]{0,1:T(8,128)(2,1)}) %all-gather.3.cloned.1.call-update) | async-done | bytes 2359312 | tf_op jit(solution)/shard_map/all_gather | solution.py:42
  63.9 4.2 convolution_convert_fusion.4
  69.2 1.7 fusion.7
  71.0 2.2 fusion.92
  73.9 64.3 %all-gather.5.cloned.1.call-done = bf16[512,7168]{0,1:T(8,128)(2,1)} async-done(((bf16[512,448]{0,1:T(8,128)(2,1)}), bf16[512,7168]{0,1:T(8,128)(2,1)}) %all-gather.5.cloned.1.call-update) | async-done | bytes 7340048 | tf_op jit(solution)/shard_map/all_gather | solution.py:69
  138.2 7.0 %convolution_convert_fusion.2 = bf16[128,7168]{1,0:T(8,128)(2,1)} fusion(bf16[128,512]{0,1:T(8,128)(2,1)S(1)} %bitcast.92, bf16[512,7168]{0,1:T(8,128)(2,1)} %all-gather.5.cloned.1.call-done), kind=kOutput, calls=%fused_computation.3 | convolution fusion | flops 940441600 | bytes 9306112 | tf_op jit(solution)/shard_map/dot_general | solution.py:67
  145.9 73.0 %reduce-scatter.2.cloned.1.call-done = bf16[8,7168]{1,0:T(8,128)(2,1)} async-done(((bf16[128,7168]{1,0:T(8,128)(2,1)}), bf16[8,7168]{1,0:T(8,128)(2,1)}) %reduce-scatter.2.cloned.1.call-update) | async-done | bytes 114704 | tf_op jit(solution)/shard_map/reduce_scatter | solution.py:72
  218.9 1.1 fusion.75
  221.5 1.3 reshape.90
  222.8 1.9 copy.46
  224.6 22.5 %all_to_all.30 = bf16[16,2,2,7168]{3,1,2,0:T(2,128)(2,1)S(1)} all-to-all(bf16[16,2,2,7168]{3,1,2,0:T(2,128)(2,1)S(1)} %copy.46), channel_id=1, replica_groups=mesh['ctx'=16,'exp'=16] {'exp'}, dimensions={0} | all-to-all | bytes 1835008 | tf_op jit(solution)/shard_map/all_to_all | solution.py:98
  248.2 90.0 %all_to_all.31 = bf16[16,32,7168]{2,1,0:T(8,128)(2,1)} all-to-all(bf16[16,32,7168]{2,1,0:T(8,128)(2,1)S(1)} %bitcast.86), channel_id=1, replica_groups=mesh['ctx'=16,'exp'=16] {'ctx'}, dimensions={0} | all-to-all | bytes 14680064 | tf_op jit(solution)/shard_map/all_to_all | solution.py:103
  338.2 1.4 broadcast_in_dim.57
  339.6 6.4 %all-to-all-start = ((bf16[16,8,7168]{2,1,0:T(8,128)(2,1)}), bf16[16,8,7168]{2,1,0:T(8,128)(2,1)}, u32[]{:S(2)}, u32[]{:S(2)}) async-start(bf16[16,8,7168]{2,1,0:T(8,128)(2,1)} %broadcast_in_dim.57), calls=%async_computation.1 | async-start | bytes 3670016 | tf_op jit(solution)/shard_map/all_to_all | solution.py:104
  346.0 5.6 %fusion.21 = f32[512,128]{1,0:T(8,128)S(1)} fusion(bf16[512,7168]{1,0:T(8,128)(2,1)} %bitcast.84, bf16[1,2,7168,128]{3,2,1,0:T(8,128)(2,1)} %param.20), kind=kOutput, calls=%fused_computation.30 | convolution fusion | flops 939524096 | bytes 9437184 | tf_op jit(solution)/shard_map/dot_general | solution.py:17
  351.7 15.4 %convolution_convert_fusion = bf16[512,7168]{1,0:T(8,128)(2,1)} fusion(bf16[1,128,7168]{2,1,0:T(8,128)(2,1)S(1)} %copy-done, bf16[512,7168]{1,0:T(8,128)(2,1)} %bitcast.85, bf16[1,2,7168,128]{3,2,1,0:T(8,128)(2,1)} %param.20, f32[512,128]{1,0:T(8,128)S(1)} %fusion.21), kind=kOutput, calls=%fused_computation.1 | convolution fusion | flops 1883111424 | bytes 18612224 | tf_op jit(solution)/shard_map/dot_general | solution.py:107
  367.0 5.1 all-to-all-done
  372.1 5.7 %all-to-all-start.4 = ((bf16[16,32,7168]{2,1,0:T(8,128)(2,1)}), bf16[16,32,7168]{2,1,0:T(8,128)(2,1)}, u32[]{:S(2)}, u32[]{:S(2)}) async-start(bf16[16,32,7168]{2,1,0:T(8,128)(2,1)} %bitcast.83), calls=%async_computation.5 | async-start | bytes 14680064 | tf_op jit(solution)/shard_map/all_to_all | solution.py:117
  377.8 2.7 fusion.25
  380.4 5.1 fusion.1
  385.5 101.1 %all-to-all-done.4 = bf16[16,32,7168]{2,1,0:T(8,128)(2,1)} async-done(((bf16[16,32,7168]{2,1,0:T(8,128)(2,1)}), bf16[16,32,7168]{2,1,0:T(8,128)(2,1)}, u32[]{:S(2)}, u32[]{:S(2)}) %all-to-all-start.4) | async-done | bytes 7340064 | tf_op jit(solution)/shard_map/all_to_all | solution.py:117
  486.6 8.8 %all-to-all-start.1 = ((bf16[16,8,7168]{2,1,0:T(8,128)(2,1)}), bf16[16,8,7168]{2,1,0:T(8,128)(2,1)}, u32[]{:S(2)}, u32[]{:S(2)}) async-start(bf16[16,8,7168]{2,1,0:T(8,128)(2,1)} %fusion.1), calls=%async_computation.2 | async-start | bytes 3670016 | tf_op jit(solution)/shard_map/all_to_all | solution.py:118
  495.5 14.9 %reshape.95 = bf16[2,8,16,2,7168]{4,3,2,1,0:T(2,128)(2,1)} reshape(bf16[16,32,7168]{2,1,0:T(8,128)(2,1)} %all-to-all-done.4) | data formatting | bytes 14680064 | tf_op jit(solution)/shard_map/reshape | solution.py:122
  510.4 8.5 %reduce = bf16[2,16,2,7168]{3,2,1,0:T(2,128)(2,1)S(1)} reduce(bf16[2,8,16,2,7168]{4,3,2,1,0:T(2,128)(2,1)} %reshape.95, bf16[]{:T(256)} %constant.44), dimensions={1}, to_apply=%region_10.11.clone | reduce | flops 3211264 | bytes 8257538 | tf_op jit(solution)/shard_map/reduce_sum | solution.py:123
  518.9 1.6 copy.48
  520.4 1.1 all-to-all-done.1
  521.5 3.6 all-to-all-start.5
  525.3 1.8 convert_reduce_fusion
  527.0 24.8 %all-to-all-done.5 = bf16[16,2,2,7168]{3,2,1,0:T(2,128)(2,1)S(1)} async-done(((bf16[16,2,2,7168]{3,2,1,0:T(2,128)(2,1)}), bf16[16,2,2,7168]{3,2,1,0:T(2,128)(2,1)S(1)}, u32[]{:S(2)}, u32[]{:S(2)}) %all-to-all-start.5) | async-done | bytes 917536 | tf_op jit(solution)/shard_map/all_to_all | solution.py:126
  551.9 1.3 reshape.97
  553.1 2.3 fusion.2
  (42 shorter events, 6.8 us)
Async XLA Ops:
  6.5 345.1 %copy-start = (bf16[1,128,7168]{2,1,0:T(8,128)(2,1)S(1)}, bf16[1,128,7168]{2,1,0:T(8,128)(2,1)}, u32[]{:S(2)}) copy-start(bf16[1,128,7168]{2,1,0:T(8,128)(2,1)} %param.21) | copy-start | bytes 5505028
  6.5 57.4 %all-gather.3.cloned.1.call-start = ((), (), s32[]{:S(2)}) async-start(), calls=%async_computation.7 | async-start | bytes 2506752 | tf_op jit(solution)/shard_map/all_gather | solution.py:42
  7.3 130.9 %all-gather.5.cloned.1.call-start = ((), (), s32[]{:S(2)}) async-start(), calls=%async_computation.8 | async-start | bytes 7798784 | tf_op jit(solution)/shard_map/all_gather | solution.py:69
  8.0 210.9 %reduce-scatter.2.cloned.1.call-start = ((), (), s32[]{:S(2)}) async-start(), calls=%async_computation.9 | async-start | bytes 1949696 | tf_op jit(solution)/shard_map/reduce_scatter | solution.py:72
  68.2 1.0 slice-start
  138.2 7.0 %copy-start.5 = (s32[8,4]{0,1:T(4,128)S(1)}, s32[8,4]{0,1:T(4,128)}, u32[]{:S(2)}) copy-start(s32[8,4]{0,1:T(4,128)} %param.18) | copy-start | bytes 388
  138.2 80.8 %copy-start.1 = (bf16[8,7168]{1,0:T(8,128)(2,1)S(1)}, bf16[8,7168]{1,0:T(8,128)(2,1)}, u32[]{:S(2)}) copy-start(bf16[8,7168]{1,0:T(8,128)(2,1)} %param.16) | copy-start | bytes 344068
  138.2 81.8 %copy-start.3 = (f32[7168]{0:T(1024)S(1)}, f32[7168]{0:T(1024)}, u32[]{:S(2)}) copy-start(f32[7168]{0:T(1024)} %param.17) | copy-start | bytes 86020
  339.6 32.5 %all-to-all-start = ((bf16[16,8,7168]{2,1,0:T(8,128)(2,1)}), bf16[16,8,7168]{2,1,0:T(8,128)(2,1)}, u32[]{:S(2)}, u32[]{:S(2)}) async-start(bf16[16,8,7168]{2,1,0:T(8,128)(2,1)} %broadcast_in_dim.57), calls=%async_computation.1 | async-start | bytes 3670016 | tf_op jit(solution)/shard_map/all_to_all | solution.py:104
  372.1 114.5 %all-to-all-start.4 = ((bf16[16,32,7168]{2,1,0:T(8,128)(2,1)}), bf16[16,32,7168]{2,1,0:T(8,128)(2,1)}, u32[]{:S(2)}, u32[]{:S(2)}) async-start(bf16[16,32,7168]{2,1,0:T(8,128)(2,1)} %bitcast.83), calls=%async_computation.5 | async-start | bytes 14680064 | tf_op jit(solution)/shard_map/all_to_all | solution.py:117
  486.6 34.9 %all-to-all-start.1 = ((bf16[16,8,7168]{2,1,0:T(8,128)(2,1)}), bf16[16,8,7168]{2,1,0:T(8,128)(2,1)}, u32[]{:S(2)}, u32[]{:S(2)}) async-start(bf16[16,8,7168]{2,1,0:T(8,128)(2,1)} %fusion.1), calls=%async_computation.2 | async-start | bytes 3670016 | tf_op jit(solution)/shard_map/all_to_all | solution.py:118
  518.9 6.3 %copy-start.4 = (f32[8,4]{0,1:T(4,128)S(1)}, f32[8,4]{0,1:T(4,128)}, u32[]{:S(2)}) copy-start(f32[8,4]{0,1:T(4,128)} %param.19) | copy-start | bytes 388
  518.9 34.3 %copy-start.2 = (bf16[8,7168]{1,0:T(8,128)(2,1)S(1)}, bf16[8,7168]{1,0:T(8,128)(2,1)}, u32[]{:S(2)}) copy-start(bf16[8,7168]{1,0:T(8,128)(2,1)} %reduce-scatter.2.cloned.1.call-done) | copy-start | bytes 344068
  521.5 30.4 %all-to-all-start.5 = ((bf16[16,2,2,7168]{3,2,1,0:T(2,128)(2,1)}), bf16[16,2,2,7168]{3,2,1,0:T(2,128)(2,1)S(1)}, u32[]{:S(2)}, u32[]{:S(2)}) async-start(bf16[16,2,2,7168]{3,2,1,0:T(2,128)(2,1)} %copy.48), calls=%async_computation.6 | async-start | bytes 1835008 | tf_op jit(solution)/shard_map/all_to_all | solution.py:126
Sparse Core Ops, SparseCore 0:
  9.9 53.9 all-gather.2
  66.7 71.4 all-gather.4
  145.3 73.6 reduce-scatter.1
where the time goes:
time: 563 us; the launch traced here: 562 us
  waiting for transfers between devices  325 us (58%)
  blocking collectives  112 us (20%)
  matrix products  45.1 us (8%)
  local copies, waits for them, and re-layouts  25.9 us (5%)
  starting transfers between devices  24.6 us (4%)
  other arithmetic  15.2 us (3%)
  between operations  13.3 us (2%)
    all_to_all x1, waiting for transfers between devices, on_device(): lax.all_to_all(routed_part, 'ctx', split_axis=0, concat_axis=0, tiled=True)  101 us
    all_to_all x1, blocking collectives, on_device(): lax.all_to_all(routed_send, 'ctx', split_axis=0, concat_axis=0, tiled=True)  90 us
    reduce_scatter x1, waiting for transfers between devices, on_device(): lax.psum_scatter(lax.optimization_barrier(projected).astype(jnp.float32)....  73 us
    all_gather x1, waiting for transfers between devices, on_device(): lax.all_gather(out_proj, 'ctx', axis=1, tiled=True)  64.3 us
    all_gather x1, waiting for transfers between devices, on_device(): shard_piece = lax.all_gather(kv_latent, 'ctx', axis=0, tiled=True)  54.6 us
    all_to_all x1, waiting for transfers between devices, on_device(): lax.all_to_all(expert_out, 'exp', split_axis=0, concat_axis=0, tiled=True)  24.8 us
    all_to_all x1, blocking collectives, on_device(): lax.all_to_all(send_rows, 'exp', split_axis=0, concat_axis=0, tiled=True)  22.5 us
    dot_general x1, matrix products, on_device(): jnp.dot(routed_act, expert_down[0], preferred_element_type=jnp.float32)  15.4 us
  transfers between devices with their start and end apart: 7, of which 7 were waited for; matrix products, arithmetic and copies ran while one was open for 12% of the time, Pallas kernels for 0%

commit v1 on v0

--- a/solution.py
+++ b/solution.py
@@ -86,9 +86,9 @@
     experts = 2 * exp_count
     capacity = min(tok_local, 2 * tok_local * TOPK // experts)
     flat_routes = routes.reshape(-1)
-    expert_ids = jnp.arange(experts, dtype=jnp.int32)
-    onehot = (flat_routes[:, None] == expert_ids[None, :]).astype(jnp.int32)
-    rank_within = jnp.sum((jnp.cumsum(onehot, axis=0) - 1) * onehot, axis=1)
+    order = jnp.arange(flat_routes.shape[0], dtype=jnp.int32)
+    earlier = (flat_routes[:, None] == flat_routes[None, :]) & (order[None, :] < order[:, None])
+    rank_within = jnp.sum(earlier.astype(jnp.int32), axis=1)
     slot_index = (flat_routes * capacity + rank_within).reshape(tok_local, TOPK)
     slot_ids = jnp.arange(experts * capacity, dtype=jnp.int32)
     matches = slot_index[None, :, :] == slot_ids[:, None, None]

time: 563 us -> 563 us (level)
  no operation moved by 1% of the time
where the time goes in v1:
time: 563 us; the launch traced here: 562 us
  waiting for transfers between devices  326 us (58%)
  blocking collectives  112 us (20%)
  matrix products  45.1 us (8%)
  local copies, waits for them, and re-layouts  25.9 us (5%)
  starting transfers between devices  24.6 us (4%)
  other arithmetic  15.1 us (3%)
  between operations  13.3 us (2%)
    all_to_all x1, waiting for transfers between devices, on_device(): lax.all_to_all(routed_part, 'ctx', split_axis=0, concat_axis=0, tiled=True)  101 us
    all_to_all x1, blocking collectives, on_device(): lax.all_to_all(routed_send, 'ctx', split_axis=0, concat_axis=0, tiled=True)  90 us
    reduce_scatter x1, waiting for transfers between devices, on_device(): lax.psum_scatter(lax.optimization_barrier(projected).astype(jnp.float32)....  73.2 us
    all_gather x1, waiting for transfers between devices, on_device(): lax.all_gather(out_proj, 'ctx', axis=1, tiled=True)  64.3 us
    all_gather x1, waiting for transfers between devices, on_device(): shard_piece = lax.all_gather(kv_latent, 'ctx', axis=0, tiled=True)  54.6 us
    all_to_all x1, waiting for transfers between devices, on_device(): lax.all_to_all(expert_out, 'exp', split_axis=0, concat_axis=0, tiled=True)  24.8 us
    all_to_all x1, blocking collectives, on_device(): lax.all_to_all(send_rows, 'exp', split_axis=0, concat_axis=0, tiled=True)  22.5 us
    dot_general x1, matrix products, on_device(): jnp.dot(routed_act, expert_down[0], preferred_element_type=jnp.float32)  15.4 us
  transfers between devices with their start and end apart: 7, of which 7 were waited for; matrix products, arithmetic and copies ran while one was open for 12% of the time, Pallas kernels for 0%

profile of v1, /device:TPU:24, one launch (start us, length us, event | category | flops | bytes accessed | tf_op | source)
XLA Modules:
  0.0 562.0 jit_solution(17232703568965402445)
XLA Ops:
  8.1 1.1 copy.41
  9.3 54.6 %all-gather.3.cloned.1.call-done = bf16[2048,576]{0,1:T(8,128)(2,1)} async-done(((bf16[128,576]{0,1:T(8,128)(2,1)}), bf16[2048,576]{0,1:T(8,128)(2,1)}) %all-gather.3.cloned.1.call-update) | async-done | bytes 2359312 | tf_op jit(solution)/shard_map/all_gather | solution.py:42
  63.9 4.2 convolution_convert_fusion.4
  69.2 1.7 fusion.7
  71.0 2.2 fusion.92
  73.9 64.3 %all-gather.5.cloned.1.call-done = bf16[512,7168]{0,1:T(8,128)(2,1)} async-done(((bf16[512,448]{0,1:T(8,128)(2,1)}), bf16[512,7168]{0,1:T(8,128)(2,1)}) %all-gather.5.cloned.1.call-update) | async-done | bytes 7340048 | tf_op jit(solution)/shard_map/all_gather | solution.py:69
  138.2 7.0 %convolution_convert_fusion.2 = bf16[128,7168]{1,0:T(8,128)(2,1)} fusion(bf16[128,512]{0,1:T(8,128)(2,1)S(1)} %bitcast.92, bf16[512,7168]{0,1:T(8,128)(2,1)} %all-gather.5.cloned.1.call-done), kind=kOutput, calls=%fused_computation.3 | convolution fusion | flops 940441600 | bytes 9306112 | tf_op jit(solution)/shard_map/dot_general | solution.py:67
  145.8 73.2 %reduce-scatter.2.cloned.1.call-done = bf16[8,7168]{1,0:T(8,128)(2,1)} async-done(((bf16[128,7168]{1,0:T(8,128)(2,1)}), bf16[8,7168]{1,0:T(8,128)(2,1)}) %reduce-scatter.2.cloned.1.call-update) | async-done | bytes 114704 | tf_op jit(solution)/shard_map/reduce_scatter | solution.py:72
  218.9 1.1 fusion.75
  221.5 1.3 reshape.91
  222.8 1.9 copy.46
  224.6 22.5 %all_to_all.30 = bf16[16,2,2,7168]{3,1,2,0:T(2,128)(2,1)S(1)} all-to-all(bf16[16,2,2,7168]{3,1,2,0:T(2,128)(2,1)S(1)} %copy.46), channel_id=1, replica_groups=mesh['ctx'=16,'exp'=16] {'exp'}, dimensions={0} | all-to-all | bytes 1835008 | tf_op jit(solution)/shard_map/all_to_all | solution.py:98
  248.2 90.0 %all_to_all.31 = bf16[16,32,7168]{2,1,0:T(8,128)(2,1)} all-to-all(bf16[16,32,7168]{2,1,0:T(8,128)(2,1)S(1)} %bitcast.86), channel_id=1, replica_groups=mesh['ctx'=16,'exp'=16] {'ctx'}, dimensions={0} | all-to-all | bytes 14680064 | tf_op jit(solution)/shard_map/all_to_all | solution.py:103
  338.2 1.4 broadcast_in_dim.58
  339.6 6.4 %all-to-all-start = ((bf16[16,8,7168]{2,1,0:T(8,128)(2,1)}), bf16[16,8,7168]{2,1,0:T(8,128)(2,1)}, u32[]{:S(2)}, u32[]{:S(2)}) async-start(bf16[16,8,7168]{2,1,0:T(8,128)(2,1)} %broadcast_in_dim.58), calls=%async_computation.1 | async-start | bytes 3670016 | tf_op jit(solution)/shard_map/all_to_all | solution.py:104
  346.0 5.6 %fusion.21 = f32[512,128]{1,0:T(8,128)S(1)} fusion(bf16[512,7168]{1,0:T(8,128)(2,1)} %bitcast.84, bf16[1,2,7168,128]{3,2,1,0:T(8,128)(2,1)} %param.20), kind=kOutput, calls=%fused_computation.30 | convolution fusion | flops 939524096 | bytes 9437184 | tf_op jit(solution)/shard_map/dot_general | solution.py:17
  351.7 15.4 %convolution_convert_fusion = bf16[512,7168]{1,0:T(8,128)(2,1)} fusion(bf16[1,128,7168]{2,1,0:T(8,128)(2,1)S(1)} %copy-done, bf16[512,7168]{1,0:T(8,128)(2,1)} %bitcast.85, bf16[1,2,7168,128]{3,2,1,0:T(8,128)(2,1)} %param.20, f32[512,128]{1,0:T(8,128)S(1)} %fusion.21), kind=kOutput, calls=%fused_computation.1 | convolution fusion | flops 1883111424 | bytes 18612224 | tf_op jit(solution)/shard_map/dot_general | solution.py:107
  367.0 5.1 all-to-all-done
  372.1 5.7 %all-to-all-start.4 = ((bf16[16,32,7168]{2,1,0:T(8,128)(2,1)}), bf16[16,32,7168]{2,1,0:T(8,128)(2,1)}, u32[]{:S(2)}, u32[]{:S(2)}) async-start(bf16[16,32,7168]{2,1,0:T(8,128)(2,1)} %bitcast.83), calls=%async_computation.5 | async-start | bytes 14680064 | tf_op jit(solution)/shard_map/all_to_all | solution.py:117
  377.8 2.7 fusion.25
  380.4 5.1 fusion.1
  385.5 101.1 %all-to-all-done.4 = bf16[16,32,7168]{2,1,0:T(8,128)(2,1)} async-done(((bf16[16,32,7168]{2,1,0:T(8,128)(2,1)}), bf16[16,32,7168]{2,1,0:T(8,128)(2,1)}, u32[]{:S(2)}, u32[]{:S(2)}) %all-to-all-start.4) | async-done | bytes 7340064 | tf_op jit(solution)/shard_map/all_to_all | solution.py:117
  486.6 8.8 %all-to-all-start.1 = ((bf16[16,8,7168]{2,1,0:T(8,128)(2,1)}), bf16[16,8,7168]{2,1,0:T(8,128)(2,1)}, u32[]{:S(2)}, u32[]{:S(2)}) async-start(bf16[16,8,7168]{2,1,0:T(8,128)(2,1)} %fusion.1), calls=%async_computation.2 | async-start | bytes 3670016 | tf_op jit(solution)/shard_map/all_to_all | solution.py:118
  495.5 14.9 %reshape.96 = bf16[2,8,16,2,7168]{4,3,2,1,0:T(2,128)(2,1)} reshape(bf16[16,32,7168]{2,1,0:T(8,128)(2,1)} %all-to-all-done.4) | data formatting | bytes 14680064 | tf_op jit(solution)/shard_map/reshape | solution.py:122
  510.4 8.5 %reduce = bf16[2,16,2,7168]{3,2,1,0:T(2,128)(2,1)S(1)} reduce(bf16[2,8,16,2,7168]{4,3,2,1,0:T(2,128)(2,1)} %reshape.96, bf16[]{:T(256)} %constant.37), dimensions={1}, to_apply=%region_9.10.clone | reduce | flops 3211264 | bytes 8257538 | tf_op jit(solution)/shard_map/reduce_sum | solution.py:123
  518.9 1.6 copy.48
  520.4 1.1 all-to-all-done.1
  521.5 3.6 all-to-all-start.5
  525.3 1.8 convert_reduce_fusion
  527.0 24.8 %all-to-all-done.5 = bf16[16,2,2,7168]{3,2,1,0:T(2,128)(2,1)S(1)} async-done(((bf16[16,2,2,7168]{3,2,1,0:T(2,128)(2,1)}), bf16[16,2,2,7168]{3,2,1,0:T(2,128)(2,1)S(1)}, u32[]{:S(2)}, u32[]{:S(2)}) %all-to-all-start.5) | async-done | bytes 917536 | tf_op jit(solution)/shard_map/all_to_all | solution.py:126
  551.9 1.3 reshape.98
  553.1 2.3 fusion.2
  (40 shorter events, 6.7 us)
Async XLA Ops:
  6.5 345.1 %copy-start = (bf16[1,128,7168]{2,1,0:T(8,128)(2,1)S(1)}, bf16[1,128,7168]{2,1,0:T(8,128)(2,1)}, u32[]{:S(2)}) copy-start(bf16[1,128,7168]{2,1,0:T(8,128)(2,1)} %param.21) | copy-start | bytes 5505028
  6.5 57.4 %all-gather.3.cloned.1.call-start = ((), (), s32[]{:S(2)}) async-start(), calls=%async_computation.7 | async-start | bytes 2506752 | tf_op jit(solution)/shard_map/all_gather | solution.py:42
  7.3 130.9 %all-gather.5.cloned.1.call-start = ((), (), s32[]{:S(2)}) async-start(), calls=%async_computation.8 | async-start | bytes 7798784 | tf_op jit(solution)/shard_map/all_gather | solution.py:69
  8.0 210.9 %reduce-scatter.2.cloned.1.call-start = ((), (), s32[]{:S(2)}) async-start(), calls=%async_computation.9 | async-start | bytes 1949696 | tf_op jit(solution)/shard_map/reduce_scatter | solution.py:72
  68.2 1.0 slice-start
  138.2 7.0 %copy-start.5 = (s32[8,4]{0,1:T(4,128)S(1)}, s32[8,4]{0,1:T(4,128)}, u32[]{:S(2)}) copy-start(s32[8,4]{0,1:T(4,128)} %param.18) | copy-start | bytes 388
  138.2 80.8 %copy-start.1 = (bf16[8,7168]{1,0:T(8,128)(2,1)S(1)}, bf16[8,7168]{1,0:T(8,128)(2,1)}, u32[]{:S(2)}) copy-start(bf16[8,7168]{1,0:T(8,128)(2,1)} %param.16) | copy-start | bytes 344068
  138.2 81.8 %copy-start.3 = (f32[7168]{0:T(1024)S(1)}, f32[7168]{0:T(1024)}, u32[]{:S(2)}) copy-start(f32[7168]{0:T(1024)} %param.17) | copy-start | bytes 86020
  339.6 32.5 %all-to-all-start = ((bf16[16,8,7168]{2,1,0:T(8,128)(2,1)}), bf16[16,8,7168]{2,1,0:T(8,128)(2,1)}, u32[]{:S(2)}, u32[]{:S(2)}) async-start(bf16[16,8,7168]{2,1,0:T(8,128)(2,1)} %broadcast_in_dim.58), calls=%async_computation.1 | async-start | bytes 3670016 | tf_op jit(solution)/shard_map/all_to_all | solution.py:104
  372.1 114.5 %all-to-all-start.4 = ((bf16[16,32,7168]{2,1,0:T(8,128)(2,1)}), bf16[16,32,7168]{2,1,0:T(8,128)(2,1)}, u32[]{:S(2)}, u32[]{:S(2)}) async-start(bf16[16,32,7168]{2,1,0:T(8,128)(2,1)} %bitcast.83), calls=%async_computation.5 | async-start | bytes 14680064 | tf_op jit(solution)/shard_map/all_to_all | solution.py:117
  486.6 34.9 %all-to-all-start.1 = ((bf16[16,8,7168]{2,1,0:T(8,128)(2,1)}), bf16[16,8,7168]{2,1,0:T(8,128)(2,1)}, u32[]{:S(2)}, u32[]{:S(2)}) async-start(bf16[16,8,7168]{2,1,0:T(8,128)(2,1)} %fusion.1), calls=%async_computation.2 | async-start | bytes 3670016 | tf_op jit(solution)/shard_map/all_to_all | solution.py:118
  518.9 6.3 %copy-start.4 = (f32[8,4]{0,1:T(4,128)S(1)}, f32[8,4]{0,1:T(4,128)}, u32[]{:S(2)}) copy-start(f32[8,4]{0,1:T(4,128)} %param.19) | copy-start | bytes 388
  518.9 34.3 %copy-start.2 = (bf16[8,7168]{1,0:T(8,128)(2,1)S(1)}, bf16[8,7168]{1,0:T(8,128)(2,1)}, u32[]{:S(2)}) copy-start(bf16[8,7168]{1,0:T(8,128)(2,1)} %reduce-scatter.2.cloned.1.call-done) | copy-start | bytes 344068
  521.5 30.4 %all-to-all-start.5 = ((bf16[16,2,2,7168]{3,2,1,0:T(2,128)(2,1)}), bf16[16,2,2,7168]{3,2,1,0:T(2,128)(2,1)S(1)}, u32[]{:S(2)}, u32[]{:S(2)}) async-start(bf16[16,2,2,7168]{3,2,1,0:T(2,128)(2,1)} %copy.48), calls=%async_computation.6 | async-start | bytes 1835008 | tf_op jit(solution)/shard_map/all_to_all | solution.py:126
Sparse Core Ops, SparseCore 0:
  9.9 53.9 all-gather.2
  66.7 71.4 all-gather.4
  145.3 73.6 reduce-scatter.1
